TPU v7x, 32 devices: a whole 2x2x4 slice. The times are simulated.
32 devices in a mesh: seq: 4 (over z), dp: 8 (over y, x, core).
Axes of the slice: x: 2, y: 2, z: 4, core: 2. Of those that a mesh axis runs over, the one named last changes fastest.
Arguments:
- tokens: bfloat16 [8, 1024, 768], P('dp', 'seq'), may hold values from -6 to 6
- qkv_weight: bfloat16 [768, 2304], P('dp'), may hold values from -0.21875 to 0.21875
- proj_weight: bfloat16 [768, 768], P('dp'), may hold values from -0.875 to 0.875
- hidden_weight: bfloat16 [768, 3072], P('dp'), may hold values from -0.21875 to 0.21875
- output_weight: bfloat16 [3072, 768], P('dp'), may hold values from -0.109375 to 0.109375
- first_gain: bfloat16 [768], P('dp'), may hold values from 0.25 to 1.75
- first_bias: bfloat16 [768], P('dp'), may hold values from -2.5 to 2.5
- second_gain: bfloat16 [768], P('dp'), may hold values from 0.25 to 1.75
- second_bias: bfloat16 [768], P('dp'), may hold values from -2.5 to 2.5
- cotangent: bfloat16 [8, 1024, 768], P('dp', 'seq'), may hold values from -6 to 6
Outputs:
- block_out: bfloat16 [8, 1024, 768], P('dp', 'seq')
- tokens_gradient: bfloat16 [8, 1024, 768], P('dp', 'seq')
- qkv_gradient: float32 [768, 2304], P('dp')
- proj_gradient: float32 [768, 768], P('dp')
- hidden_gradient: float32 [768, 3072], P('dp')
- output_gradient: float32 [3072, 768], P('dp')
- first_gain_gradient: float32 [768], P('dp')
- first_bias_gradient: float32 [768], P('dp')
- second_gain_gradient: float32 [768], P('dp')
- second_bias_gradient: float32 [768], P('dp')
All inputs are finite; a program needn't handle non-finite values.
Results may differ from a plain program's by a relative error of at most 0.012.
Values may be sent and summed in bfloat16 or wider, within the bound.
A program may use at most 256 MiB of HBM per device.

v0:
```python
import jax
import jax.numpy as jnp
from jax import lax
from jax.sharding import PartitionSpec as P

HEAD_DIM = 64
LOW = jnp.bfloat16
F32 = jnp.float32


def layer_norm(values, gain, bias):
    average = jnp.mean(values, -1, keepdims=True)
    centred = values - average
    variance = jnp.mean(centred * centred, -1, keepdims=True)
    return centred * lax.rsqrt(variance + 1e-05) * gain + bias


def gelu_tanh(values):
    return jax.nn.gelu(values, approximate=True)


def matmul(left, right):
    return jnp.dot(left, right, preferred_element_type=F32)


def matmul_left_t(left, right):
    return lax.dot_general(left, right, (((0,), (0,)), ((), ())), preferred_element_type=F32)


def matmul_right_t(left, right):
    return lax.dot_general(left, right, (((1,), (1,)), ((), ())), preferred_element_type=F32)


def gather_seq(value):
    return lax.all_gather(value, "seq", axis=0, tiled=True)


def scatter_seq(value):
    return lax.psum_scatter(value.astype(LOW), "seq", scatter_dimension=0, tiled=True).astype(F32)


def attention_forward(queries, keys, values):
    length, local_width = queries.shape
    heads_here = local_width // HEAD_DIM
    block_rows = min(512, length)
    blocks = length // block_rows
    scale = HEAD_DIM ** (-0.5)
    outs, logs = ([], [])
    key_index = jnp.arange(length)
    for b in range(blocks):
        seen = (b + 1) * block_rows
        q = queries[b * block_rows : seen].reshape(block_rows, heads_here, HEAD_DIM)
        k = keys[:seen].reshape(seen, heads_here, HEAD_DIM)
        v = values[:seen].reshape(seen, heads_here, HEAD_DIM)
        raw = jnp.einsum("qhd,khd->hqk", q, k, preferred_element_type=F32)
        positions = b * block_rows + jnp.arange(block_rows)
        causal = key_index[None, :seen] <= positions[:, None]
        scores = jnp.where(causal[None], raw * scale, -1e30)
        largest = jnp.max(scores, -1, keepdims=True)
        expo = jnp.exp(scores - largest)
        total = jnp.sum(expo, -1, keepdims=True)
        probs = (expo / total).astype(LOW)
        context = jnp.einsum("hqk,khd->qhd", probs, v, preferred_element_type=F32)
        outs.append(context.astype(LOW).reshape(block_rows, local_width))
        logs.append(largest + jnp.log(total))
    return (jnp.concatenate(outs, axis=0), logs)


def attention_backward(queries, keys, values, grads, logs):
    length, local_width = queries.shape
    heads_here = local_width // HEAD_DIM
    block_rows = min(512, length)
    blocks = length // block_rows
    scale = HEAD_DIM ** (-0.5)
    key_index = jnp.arange(length)
    query_grads = []
    key_sum = jnp.zeros((length, heads_here, HEAD_DIM), F32)
    value_sum = jnp.zeros((length, heads_here, HEAD_DIM), F32)
    for b in range(blocks):
        seen = (b + 1) * block_rows
        q = queries[b * block_rows : seen].reshape(block_rows, heads_here, HEAD_DIM)
        g = grads[b * block_rows : seen].reshape(block_rows, heads_here, HEAD_DIM)
        k = keys[:seen].reshape(seen, heads_here, HEAD_DIM)
        v = values[:seen].reshape(seen, heads_here, HEAD_DIM)
        raw = jnp.einsum("qhd,khd->hqk", q, k, preferred_element_type=F32)
        positions = b * block_rows + jnp.arange(block_rows)
        causal = key_index[None, :seen] <= positions[:, None]
        scores = jnp.where(causal[None], raw * scale, -1e30)
        probs = jnp.exp(scores - logs[b])
        low_probs = probs.astype(LOW)
        value_term = jnp.einsum("hqk,qhd->khd", low_probs, g, preferred_element_type=F32)
        prob_grad = jnp.einsum("qhd,khd->hqk", g, v, preferred_element_type=F32)
        score_grad = (probs * (prob_grad - jnp.sum(probs * prob_grad, -1, keepdims=True))).astype(
            LOW
        )
        query_grad = jnp.einsum("hqk,khd->qhd", score_grad, k, preferred_element_type=F32) * scale
        key_term = jnp.einsum("hqk,qhd->khd", score_grad, q, preferred_element_type=F32) * scale
        pad = ((0, length - seen), (0, 0), (0, 0))
        key_sum = key_sum + jnp.pad(key_term, pad)
        value_sum = value_sum + jnp.pad(value_term, pad)
        query_grads.append(query_grad.astype(LOW).reshape(block_rows, local_width))
    return (
        jnp.concatenate(query_grads, axis=0),
        key_sum.astype(LOW).reshape(length, local_width),
        value_sum.astype(LOW).reshape(length, local_width),
    )


def on_device(
    tokens,
    qkv_weight,
    proj_weight,
    hidden_weight,
    output_weight,
    first_gain,
    first_bias,
    second_gain,
    second_bias,
    cotangent,
):
    parts = lax.axis_size("seq")
    groups = lax.axis_size("dp")
    part = lax.axis_index("seq")
    inputs_low = tokens[0]
    rows, width = inputs_low.shape
    model_rows = qkv_weight.shape[0]
    local_width = width // parts
    hidden_rows = output_weight.shape[0] // parts
    hidden_here = hidden_rows * groups
    qkv_here = lax.dynamic_index_in_dim(
        qkv_weight.reshape(model_rows, 3, parts, local_width), part, 2, keepdims=False
    ).reshape(model_rows, 3 * local_width)
    hidden_cols = lax.dynamic_index_in_dim(
        hidden_weight.reshape(model_rows, groups, parts, hidden_rows), part, 2, keepdims=False
    ).reshape(model_rows, hidden_here)
    output_here = lax.dynamic_slice_in_dim(output_weight, part * hidden_rows, hidden_rows, 0)
    norms = jnp.stack([first_gain, first_bias, second_gain, second_bias], axis=0)
    norms = lax.all_gather(norms, "dp", axis=1, tiled=True).astype(F32)
    gain_one, bias_one, gain_two, bias_two = (norms[0], norms[1], norms[2], norms[3])
    all_tokens = gather_seq(inputs_low)
    wide_qkv = lax.all_gather(qkv_here, "dp", axis=0, tiled=True)
    wide_proj = lax.all_gather(proj_weight, "dp", axis=0, tiled=True)
    wide_hidden = lax.all_gather(hidden_cols, "dp", axis=0, tiled=True)
    wide_output = lax.all_gather(output_here, "dp", axis=0, tiled=True)
    all_grads = gather_seq(cotangent[0])
    inputs = all_tokens.astype(F32)
    lowered_one = layer_norm(inputs, gain_one, bias_one).astype(LOW)
    projected = matmul(lowered_one, wide_qkv).astype(LOW)
    queries = projected[:, :local_width]
    keys = projected[:, local_width : 2 * local_width]
    values = projected[:, 2 * local_width :]
    context_here, logs = attention_forward(queries, keys, values)
    context = lax.all_gather(context_here, "seq", axis=1, tiled=True)
    middle = inputs + matmul(context, wide_proj)
    lowered_two = layer_norm(middle, gain_two, bias_two).astype(LOW)
    hidden_pre = matmul(lowered_two, wide_hidden)
    activated_float, gelu_pull = jax.vjp(gelu_tanh, hidden_pre)
    activated = activated_float.astype(LOW)
    act_grad = matmul_right_t(all_grads, wide_output)
    pre_grad = gelu_pull(act_grad)[0].astype(LOW)
    normed_two_grad = scatter_seq(matmul_right_t(pre_grad, wide_hidden))
    ffn_out = scatter_seq(matmul(activated, wide_output))
    middle_own = lax.dynamic_slice_in_dim(middle, part * rows, rows, 0)
    block_out = middle_own + ffn_out
    _, norm_pull_two = jax.vjp(layer_norm, middle_own, gain_two, bias_two)
    middle_part, gain_two_term, bias_two_term = norm_pull_two(normed_two_grad)
    middle_grad = cotangent[0].astype(F32) + middle_part
    attn_grad = gather_seq(middle_grad.astype(LOW))
    proj_here = lax.dynamic_slice_in_dim(wide_proj, part * local_width, local_width, 0)
    context_grad = matmul_right_t(attn_grad, proj_here).astype(LOW)
    query_grads, key_grads, value_grads = attention_backward(
        queries, keys, values, context_grad, logs
    )
    qkv_grad = jnp.concatenate([query_grads, key_grads, value_grads], axis=1)
    normed_one_grad = scatter_seq(matmul_right_t(qkv_grad, wide_qkv))
    _, norm_pull_one = jax.vjp(layer_norm, inputs_low.astype(F32), gain_one, bias_one)
    input_part, gain_one_term, bias_one_term = norm_pull_one(normed_one_grad)
    tokens_gradient = (middle_grad + input_part).astype(LOW)
    attn_cols = lax.dynamic_slice_in_dim(attn_grad, part * local_width, local_width, 1)
    output_term = matmul_left_t(activated, all_grads).astype(LOW)
    hidden_term = matmul_left_t(lowered_two, pre_grad).astype(LOW)
    proj_term = matmul_left_t(context, attn_cols).astype(LOW)
    qkv_term = matmul_left_t(lowered_one, qkv_grad).astype(LOW)
    first_terms = jnp.concatenate([output_term, hidden_term], axis=1)
    second_terms = jnp.concatenate([proj_term, qkv_term], axis=1)
    first_sum = lax.psum_scatter(first_terms, "dp", scatter_dimension=0, tiled=True)
    second_sum = lax.psum_scatter(second_terms, "dp", scatter_dimension=0, tiled=True)
    first_all = lax.all_gather(first_sum, "seq", axis=0)
    second_all = lax.all_gather(second_sum, "seq", axis=0)
    output_gradient = first_all[:, :, :width].reshape(parts * hidden_rows, width).astype(F32)
    hidden_gradient = (
        first_all[:, :, width:]
        .reshape(parts, model_rows, groups, hidden_rows)
        .transpose(1, 2, 0, 3)
        .reshape(model_rows, parts * hidden_here)
        .astype(F32)
    )
    proj_gradient = (
        second_all[:, :, :local_width].transpose(1, 0, 2).reshape(model_rows, width).astype(F32)
    )
    qkv_gradient = (
        second_all[:, :, local_width:]
        .reshape(parts, model_rows, 3, local_width)
        .transpose(1, 2, 0, 3)
        .reshape(model_rows, 3 * width)
        .astype(F32)
    )
    norm_terms = jnp.stack([gain_one_term, bias_one_term, gain_two_term, bias_two_term], axis=0)
    norm_sum = lax.psum(norm_terms, ("seq", "dp"))
    norm_own = lax.dynamic_slice_in_dim(
        norm_sum, lax.axis_index("dp") * first_gain.shape[0], first_gain.shape[0], 1
    )
    return (
        block_out.astype(LOW)[None],
        tokens_gradient[None],
        qkv_gradient,
        proj_gradient,
        hidden_gradient,
        output_gradient,
        norm_own[0],
        norm_own[1],
        norm_own[2],
        norm_own[3],
    )


def solution(mesh):
    placed = (
        P("dp", "seq", None),
        P("dp", None),
        P("dp", None),
        P("dp", None),
        P("dp", None),
        P("dp"),
        P("dp"),
        P("dp"),
        P("dp"),
        P("dp", "seq", None),
    )
    return jax.shard_map(
        on_device,
        mesh=mesh,
        in_specs=placed,
        out_specs=(
            P("dp", "seq", None),
            P("dp", "seq", None),
            P("dp", None),
            P("dp", None),
            P("dp", None),
            P("dp", None),
            P("dp"),
            P("dp"),
            P("dp"),
            P("dp"),
        ),
        check_vma=False,
    )
```

profile of v0, /device:TPU:0, one launch (start us, length us, event | category | flops | bytes accessed | tf_op | source)
XLA Modules:
  0.0 499.9 jit_solution(855848961846258834)
XLA Ops:
  7.2 2.0 copy.123
  10.8 10.3 %all-gather.4 = bf16[8,96,4]{1,2,0:T(4,128)(2,1)S(1)} all-gather(bf16[1,96,4]{1,2,0:T(4,128)(2,1)S(1)} %maximum_bitcast_fusion), channel_id=1, replica_groups=mesh['seq'=4,'dp'=8] {'dp'}, dimensions={0}, use_global_device_ids=true | all-gather | bytes 6912 | tf_op jit(solution)/shard_map/all_gather | solution.py:138
  22.4 1.6 reshape.258
  24.7 11.9 %all_gather.41 = bf16[768,576]{1,0:T(8,128)(2,1)} all-gather(bf16[96,576]{1,0:T(8,128)(2,1)S(1)} %copy.126), channel_id=1, replica_groups=mesh['seq'=4,'dp'=8] {'dp'}, dimensions={0}, use_global_device_ids=true | all-gather | bytes 995328 | tf_op jit(solution)/shard_map/all_gather | solution.py:141
  36.7 13.9 %all-gather.24.cloned.1.call-done = bf16[1,1024,768]{1,2,0:T(8,128)(2,1)} async-done(((bf16[1,256,768]{1,2,0:T(8,128)(2,1)}), bf16[1,1024,768]{1,2,0:T(8,128)(2,1)}) %all-gather.24.cloned.1.call-update) | async-done | bytes 1572880 | tf_op jit(solution)/shard_map/all_gather | solution.py:35
  50.6 1.8 convert_reduce_fusion
  52.5 1.9 fusion.6
  54.9 1.3 convolution_convert_fusion.4
  57.2 1.4 fusion.88
  59.2 1.5 fusion
  61.7 1.7 fusion.55
  65.5 1.2 dynamic-slice_reduce_fusion.1
  69.1 5.8 %all-gather.16.cloned.1.call-done = bf16[768,768]{1,0:T(8,128)(2,1)} async-done(((bf16[96,768]{1,0:T(8,128)(2,1)}), bf16[768,768]{1,0:T(8,128)(2,1)}) %all-gather.16.cloned.1.call-update) | async-done | bytes 1179664 | tf_op jit(solution)/shard_map/all_gather | solution.py:142
  74.8 39.3 %all-gather.14.cloned.1.call-done = bf16[1024,768]{0,1:T(8,128)(2,1)} async-done(((bf16[1024,192]{0,1:T(8,128)(2,1)}), bf16[1024,768]{0,1:T(8,128)(2,1)}) %all-gather.14.cloned.1.call-update) | async-done | bytes 1572880 | tf_op jit(solution)/shard_map/all_gather | solution.py:153
  114.1 3.7 fusion.90
  118.5 1.7 add_convert_fusion
  120.2 19.2 %all-gather.18.cloned.1.call-done = bf16[768,768]{1,0:T(8,128)(2,1)} async-done(((bf16[96,768]{1,0:T(8,128)(2,1)}), bf16[768,768]{1,0:T(8,128)(2,1)}) %all-gather.18.cloned.1.call-update) | async-done | bytes 1179664 | tf_op jit(solution)/shard_map/all_gather | solution.py:143
  139.4 4.8 fusion.91
  144.2 21.0 %all-gather.20.cloned.1.call-done = bf16[768,768]{1,0:T(8,128)(2,1)} async-done(((bf16[96,768]{1,0:T(8,128)(2,1)}), bf16[768,768]{1,0:T(8,128)(2,1)}) %all-gather.20.cloned.1.call-update) | async-done | bytes 1179664 | tf_op jit(solution)/shard_map/all_gather | solution.py:144
  165.2 38.5 %all-gather.26.cloned.1.call-done = bf16[1,1024,768]{2,1,0:T(8,128)(2,1)} async-done(((bf16[1,256,768]{2,1,0:T(8,128)(2,1)}), bf16[1,1024,768]{2,1,0:T(8,128)(2,1)}) %all-gather.26.cloned.1.call-update) | async-done | bytes 1572880 | tf_op jit(solution)/shard_map/all_gather | solution.py:35
  203.8 5.6 %fusion.16 = bf16[1024,768]{1,0:T(8,128)(2,1)S(1)} fusion(f32[1024,768]{1,0:T(8,128)} %fusion.91, bf16[768,768]{1,0:T(8,128)(2,1)} %all-gather.20.cloned.1.call-done, bf16[1,1024,768]{2,1,0:T(8,128)(2,1)} %all-gather.26.cloned.1.call-done), kind=kOutput, calls=%fused_computation.26 | convolution fusion | flops 1223688192 | bytes 7471104 | tf_op jit(solution)/shard_map/dot_general | solution.py:31
  209.4 1.1 copy-done.55
  210.5 2.6 convolution_convert_fusion.1
  213.4 3.5 convolution_convert_fusion.3
  216.9 1.7 fusion.33
  218.6 1.5 pad_maximum_fusion
  220.2 4.3 copy.156
  224.6 1.9 copy.130
  227.2 20.3 %reduce-scatter.12.cloned.1.call-done = bf16[256,768]{0,1:T(8,128)(2,1)} async-done(((bf16[1024,768]{0,1:T(8,128)(2,1)}), bf16[256,768]{0,1:T(8,128)(2,1)}) %reduce-scatter.12.cloned.1.call-update) | async-done | bytes 393232 | tf_op jit(solution)/shard_map/reduce_scatter | solution.py:39
  247.5 2.0 multiply_reduce_fusion.3
  249.5 2.1 fusion.67
  252.2 2.7 fusion.70
  255.0 1.3 log_add_fusion.1
  257.0 35.3 %reduce-scatter.18.cloned.1.call-done = bf16[96,1536]{1,0:T(8,128)(2,1)} async-done(((bf16[768,1536]{1,0:T(8,128)(2,1)}), bf16[96,1536]{1,0:T(8,128)(2,1)}) %reduce-scatter.18.cloned.1.call-update) | async-done | bytes 294928 | tf_op jit(solution)/shard_map/reduce_scatter | solution.py:186
  292.4 39.9 %all-gather.22.cloned.1.call-done = bf16[1024,768]{0,1:T(8,128)(2,1)} async-done(((bf16[256,768]{0,1:T(8,128)(2,1)}), bf16[1024,768]{0,1:T(8,128)(2,1)}) %all-gather.22.cloned.1.call-update) | async-done | bytes 1572880 | tf_op jit(solution)/shard_map/all_gather | solution.py:35
  332.3 2.0 convolution_convert_fusion.6
  334.4 1.5 multiply_reduce_fusion.1
  339.3 1.9 multiply_reduce_fusion
  341.2 1.4 multiply_convert_fusion
  342.6 1.1 fusion.53
  344.0 1.7 convolution_convert_fusion.7
  347.1 1.2 fusion.45
  348.5 1.3 convolution_convert_fusion.5
  349.9 1.5 copy.154
  351.5 2.5 convolution_convert_fusion
  354.3 5.0 %convolution_convert_fusion.2 = bf16[1024,768]{0,1:T(8,128)(2,1)} fusion(bf16[768,768]{1,0:T(8,128)(2,1)} %all-gather.20.cloned.1.call-done, f32[1024,768]{1,0:T(8,128)} %fusion.91), kind=kOutput, calls=%fused_computation.50 | convolution fusion | flops 1215823872 | bytes 5898240 | tf_op jit(solution)/shard_map/dot_general | solution.py:23
  361.3 1.2 all-gather.28.cloned.1.call-done
  362.5 2.4 fusion.84
  364.9 1.9 reshape.285
  366.9 2.2 copy.143
  369.0 3.6 reshape.282
  372.6 1.1 bitcast_convert_fusion
  373.8 28.3 %reduce-scatter.16.cloned.1.call-done = bf16[96,768]{1,0:T(8,128)(2,1)} async-done(((bf16[768,768]{1,0:T(8,128)(2,1)}), bf16[96,768]{1,0:T(8,128)(2,1)}) %reduce-scatter.16.cloned.1.call-update) | async-done | bytes 147472 | tf_op jit(solution)/shard_map/reduce_scatter | solution.py:187
  402.0 22.2 %all-gather.2 = bf16[384,768]{1,0:T(8,128)(2,1)S(1)} all-gather(bf16[96,768]{1,0:T(8,128)(2,1)} %reduce-scatter.16.cloned.1.call-done), channel_id=4, replica_groups=mesh['seq'=4,'dp'=8] {'seq'}, dimensions={0}, use_global_device_ids=true | all-gather | bytes 737280 | tf_op jit(solution)/shard_map/all_gather | solution.py:189
  424.5 1.0 reshape.281
  426.2 1.5 copy.140
  427.8 2.9 reshape.280
  430.7 13.6 %reduce-scatter.14.cloned.1.call-done = bf16[256,768]{0,1:T(8,128)(2,1)} async-done(((bf16[1024,768]{0,1:T(8,128)(2,1)}), bf16[256,768]{0,1:T(8,128)(2,1)}) %reduce-scatter.14.cloned.1.call-update) | async-done | bytes 393232 | tf_op jit(solution)/shard_map/reduce_scatter | solution.py:39
  444.3 1.4 fusion.66
  445.8 1.5 fusion.68
  447.3 41.4 %psum.7 = f32[4,768]{1,0:T(4,128)S(1)} all-reduce(f32[4,768]{1,0:T(4,128)S(1)} %pad_maximum_fusion.6), channel_id=1, replica_groups=mesh['seq'=4,'dp'=8] {'seq','dp'}, use_global_device_ids=true, to_apply=%region_27.28 | all-reduce | flops 3072 | bytes 24576 | tf_op jit(solution)/shard_map/psum | solution.py:209
  489.3 2.0 fusion.73
  491.3 0.9 copy.145
  492.3 0.9 copy.144
  (196 shorter events, 23.0 us)
Async XLA Ops:
  7.2 60.5 %copy-start = (bf16[384,768]{1,0:T(8,128)(2,1)S(1)}, bf16[384,768]{1,0:T(8,128)(2,1)}, u32[]{:S(2)}) copy-start(bf16[384,768]{1,0:T(8,128)(2,1)} %param.14) | copy-start | bytes 1769476
  7.2 43.4 %all-gather.24.cloned.1.call-start = ((), (), s32[]{:S(2)}) async-start(), calls=%async_computation.13 | async-start | bytes 1966080 | tf_op jit(solution)/shard_map/all_gather | solution.py:35
  9.2 65.6 %all-gather.16.cloned.1.call-start = ((), (), s32[]{:S(2)}) async-start(), calls=%async_computation.6 | async-start | bytes 1327104 | tf_op jit(solution)/shard_map/all_gather | solution.py:142
  10.0 104.1 %all-gather.14.cloned.1.call-start = ((), (), s32[]{:S(2)}) async-start(), calls=%async_computation.5 | async-start | bytes 1966080 | tf_op jit(solution)/shard_map/all_gather | solution.py:153
  21.8 32.5 %copy-start.47 = (f32[768]{0:T(1024)}, f32[768]{0:T(1024)S(1)}, u32[]{:S(2)}) copy-start(f32[768]{0:T(1024)S(1)} %get-tuple-element.82) | copy-start | bytes 9220
  50.6 4.3 copy-start.7
  50.6 4.3 copy-start.19
  52.4 3.8 copy-start.36
  56.3 2.3 copy-start.11
  56.4 2.3 copy-start.13
  56.4 2.3 copy-start.15
  56.4 4.3 copy-start.21
  56.4 5.2 %copy-start.17 = (bf16[1024,192]{0,1:T(8,128)(2,1)}, bf16[1024,192]{0,1:T(8,128)(2,1)S(1)}, u32[]{:S(2)}) copy-start(bf16[1024,192]{0,1:T(8,128)(2,1)S(1)} %get-tuple-element.93) | copy-start | bytes 1179652
  57.2 3.5 copy-start.3
  58.7 3.0 copy-start.2
  58.7 3.0 copy-start.29
  59.2 1.8 copy-start.31
  61.7 3.0 copy-start.23
  64.2 75.2 %all-gather.18.cloned.1.call-start = ((), (), s32[]{:S(2)}) async-start(), calls=%async_computation.7 | async-start | bytes 1327104 | tf_op jit(solution)/shard_map/all_gather | solution.py:143
  67.6 97.6 %all-gather.20.cloned.1.call-start = ((), (), s32[]{:S(2)}) async-start(), calls=%async_computation.8 | async-start | bytes 1327104 | tf_op jit(solution)/shard_map/all_gather | solution.py:144
  68.4 135.3 %all-gather.26.cloned.1.call-start = ((), (), s32[]{:S(2)}) async-start(), calls=%async_computation.14 | async-start | bytes 1966080 | tf_op jit(solution)/shard_map/all_gather | solution.py:35
  69.0 178.5 %reduce-scatter.12.cloned.1.call-start = ((), (), s32[]{:S(2)}) async-start(), calls=%async_computation.10 | async-start | bytes 1966080 | tf_op jit(solution)/shard_map/reduce_scatter | solution.py:39
  117.9 131.6 %copy-start.5 = (f32[1024,768]{0,1:T(8,128)}, f32[1024,768]{0,1:T(8,128)S(1)}, u32[]{:S(2)}) copy-start(f32[1024,768]{0,1:T(8,128)S(1)} %get-tuple-element.109) | copy-start | bytes 9437188
  203.8 6.8 %copy-start.53 = (bf16[768,768]{1,0:T(8,128)(2,1)S(1)}, bf16[768,768]{1,0:T(8,128)(2,1)}, u32[]{:S(2)}) copy-start(bf16[768,768]{1,0:T(8,128)(2,1)} %all-gather.18.cloned.1.call-done) | copy-start | bytes 3538948
  213.2 79.1 %reduce-scatter.18.cloned.1.call-start = ((), (), s32[]{:S(2)}) async-start(), calls=%async_computation.17 | async-start | bytes 2654208 | tf_op jit(solution)/shard_map/reduce_scatter | solution.py:186
  213.4 3.5 copy-start.52
  213.4 3.5 copy-start.54
  224.5 107.8 %all-gather.22.cloned.1.call-start = ((), (), s32[]{:S(2)}) async-start(), calls=%async_computation.11 | async-start | bytes 1966080 | tf_op jit(solution)/shard_map/all_gather | solution.py:35
  249.5 2.1 copy-start.39
  249.5 2.1 copy-start.41
  251.6 82.8 %copy-start.4 = (f32[3,512,512]{1,2,0:T(8,128)S(1)}, f32[3,512,512]{1,2,0:T(8,128)}, u32[]{:S(2)}) copy-start(f32[3,512,512]{1,2,0:T(8,128)} %copy-done.3) | copy-start | bytes 9437188
  254.9 107.6 %all-gather.28.cloned.1.call-start = ((), (), s32[]{:S(2)}) async-start(), calls=%async_computation.15 | async-start | bytes 1474560 | tf_op jit(solution)/shard_map/all_gather | solution.py:188
  292.3 109.7 %reduce-scatter.16.cloned.1.call-start = ((), (), s32[]{:S(2)}) async-start(), calls=%async_computation.16 | async-start | bytes 1327104 | tf_op jit(solution)/shard_map/reduce_scatter | solution.py:187
  332.3 2.1 copy-start.22
  334.4 1.5 copy-start.28
  335.9 2.4 slice-start
  335.9 1.5 copy-start.14
  335.9 3.1 slice-start.1
  337.0 2.3 copy-start.18
  337.4 10.9 %copy-start.26 = (bf16[3,64,512]{2,1,0:T(8,128)(2,1)}, bf16[3,64,512]{2,1,0:T(8,128)(2,1)S(1)}, u32[]{:S(2)}) copy-start(bf16[3,64,512]{2,1,0:T(8,128)(2,1)S(1)} %fusion.52) | copy-start | bytes 589828
  342.6 3.2 copy-start.12
  344.0 4.3 copy-start.24
  347.1 1.4 copy-start.8
  347.1 1.4 copy-start.37
  347.1 1.4 copy-start.48
  347.1 1.4 copy-start.50
  349.8 1.7 copy-start.20
  349.8 1.7 copy-start.25
  349.8 1.7 copy-start.27
  351.4 92.9 %reduce-scatter.14.cloned.1.call-start = ((), (), s32[]{:S(2)}) async-start(), calls=%async_computation.12 | async-start | bytes 1966080 | tf_op jit(solution)/shard_map/reduce_scatter | solution.py:39
  354.1 5.4 %copy-start.6 = (bf16[1,256,768]{1,2,0:T(8,128)(2,1)S(1)}, bf16[1,256,768]{1,2,0:T(8,128)(2,1)}, u32[]{:S(2)}) copy-start(bf16[1,256,768]{1,2,0:T(8,128)(2,1)} %copy.123) | copy-start | bytes 1179652
  354.1 6.0 %copy-start.34 = (f32[768]{0:T(1024)S(1)}, f32[768]{0:T(1024)}, u32[]{:S(2)}) copy-start(f32[768]{0:T(1024)} %get-tuple-element.79) | copy-start | bytes 9220
  354.1 6.6 %copy-start.35 = (f32[768]{0:T(1024)S(1)}, f32[768]{0:T(1024)}, u32[]{:S(2)}) copy-start(f32[768]{0:T(1024)} %get-tuple-element.70) | copy-start | bytes 9220
  354.1 135.2 %reduce-scatter.10.cloned.1.call-start = ((), (), s32[]{:S(2)}) async-start(), calls=%async_computation.9 | async-start | bytes 1966080 | tf_op jit(solution)/shard_map/reduce_scatter | solution.py:39
  426.1 18.2 %copy-start.38 = (f32[256]{0:T(256)S(1)}, f32[256]{0:T(256)}, u32[]{:S(2)}) copy-start(f32[256]{0:T(256)} %broadcast_multiply_fusion.2) | copy-start | bytes 3076
  426.1 21.1 %copy-start.43 = (f32[1,768]{1,0:T(1,128)S(1)}, f32[1,768]{1,0:T(1,128)}, u32[]{:S(2)}) copy-start(f32[1,768]{1,0:T(1,128)} %reshape.279) | copy-start | bytes 9220
  426.1 21.1 %copy-start.44 = (f32[1,768]{1,0:T(1,128)S(1)}, f32[1,768]{1,0:T(1,128)}, u32[]{:S(2)}) copy-start(f32[1,768]{1,0:T(1,128)} %reshape.278) | copy-start | bytes 9220
  426.2 63.1 %copy-start.9 = (bf16[256,768]{0,1:T(8,128)(2,1)S(1)}, bf16[256,768]{0,1:T(8,128)(2,1)}, u32[]{:S(2)}) copy-start(bf16[256,768]{0,1:T(8,128)(2,1)} %reduce-scatter.12.cloned.1.call-done) | copy-start | bytes 1179652
  426.2 63.1 %copy-start.10 = (bf16[1,256,768]{1,2,0:T(8,128)(2,1)S(1)}, bf16[1,256,768]{1,2,0:T(8,128)(2,1)}, u32[]{:S(2)}) copy-start(bf16[1,256,768]{1,2,0:T(8,128)(2,1)} %copy.130) | copy-start | bytes 1179652
  426.2 63.1 %copy-start.32 = (f32[256]{0:T(256)S(1)}, f32[256]{0:T(256)}, u32[]{:S(2)}) copy-start(f32[256]{0:T(256)} %broadcast_multiply_fusion.3) | copy-start | bytes 3076
  426.2 63.1 %copy-start.40 = (f32[256]{0:T(256)S(1)}, f32[256]{0:T(256)}, u32[]{:S(2)}) copy-start(f32[256]{0:T(256)} %copy-done.39) | copy-start | bytes 3076
  426.2 63.1 %copy-start.42 = (f32[256]{0:T(256)S(1)}, f32[256]{0:T(256)}, u32[]{:S(2)}) copy-start(f32[256]{0:T(256)} %copy-done.41) | copy-start | bytes 3076
  426.2 63.1 %copy-start.46 = (f32[256]{0:T(256)S(1)}, f32[256]{0:T(256)}, u32[]{:S(2)}) copy-start(f32[256]{0:T(256)} %copy-done.45) | copy-start | bytes 3076
  444.3 48.9 %copy-start.1 = (bf16[384,768]{1,0:T(8,128)(2,1)S(1)}, bf16[384,768]{1,0:T(8,128)(2,1)}, u32[]{:S(2)}) copy-start(bf16[384,768]{1,0:T(8,128)(2,1)} %param.14) | copy-start | bytes 1769476
  (7 other events, 6.5 us)
Sparse Core Ops, SparseCore 0:
  10.2 40.3 all-gather.23
  52.5 22.3 all-gather.15
  77.0 37.0 all-gather.13
  116.4 22.9 all-gather.17
  141.1 24.0 all-gather.19
  166.6 37.0 all-gather.25
  213.3 34.1 reduce-scatter.11
  250.8 41.4 reduce-scatter.17
  294.5 37.6 all-gather.21
  333.8 28.7 all-gather.27
  366.1 35.8 reduce-scatter.15
  404.2 40.0 reduce-scatter.13
  446.6 35.2 reduce-scatter.9
where the time goes:
time: 508 us; the launch traced here: 500 us
  waiting for transfers between devices  278 us (55%)
  blocking collectives  85.8 us (17%)
  matrix products  48.4 us (10%)
  local copies, waits for them, and re-layouts  38.9 us (8%)
  other arithmetic  32.6 us (6%)
  between operations  15.1 us (3%)
    all_gather x3, waiting for transfers between devices, gather_seq(): return lax.all_gather(value, 'seq', axis=0, tiled=True)  92.4 us
    psum x1, blocking collectives, on_device(): norm_sum = lax.psum(norm_terms, ('seq', 'dp'))  41.4 us
    all_gather x1, waiting for transfers between devices, on_device(): context = lax.all_gather(context_here, 'seq', axis=1, tiled=True)  39.3 us
    reduce_scatter x1, waiting for transfers between devices, on_device(): lax.psum_scatter(first_terms, 'dp', scatter_dimension=0, tiled=True)  35.3 us
    reduce_scatter x3, waiting for transfers between devices, scatter_seq(): lax.psum_scatter(value.astype(LOW), 'seq', scatter_dimension=0, tiled=True)  33.9 us
    reduce_scatter x1, waiting for transfers between devices, on_device(): lax.psum_scatter(second_terms, 'dp', scatter_dimension=0, tiled=True)  28.3 us
    all_gather x1, blocking collectives, on_device(): second_all = lax.all_gather(second_sum, 'seq', axis=0)  22.2 us
    all_gather x1, waiting for transfers between devices, on_device(): wide_output = lax.all_gather(output_here, 'dp', axis=0, tiled=True)  21 us
  transfers between devices with their start and end apart: 13, of which 12 were waited for; matrix products, arithmetic and copies ran while one was open for 20% of the time, Pallas kernels for 0%

commit v1 on v0

--- a/solution.py
+++ b/solution.py
@@ -150,7 +150,21 @@
     keys = projected[:, local_width : 2 * local_width]
     values = projected[:, 2 * local_width :]
     context_here, logs = attention_forward(queries, keys, values)
-    context = lax.all_gather(context_here, "seq", axis=1, tiled=True)
+    ways, here, step = (lax.axis_size("seq"), lax.axis_index("seq"), context_here.shape[1])
+    shape = [n * ways if d == 1 else n for d, n in enumerate(context_here.shape)]
+    full = lax.dynamic_update_slice_in_dim(
+        jnp.zeros(shape, context_here.dtype), context_here, here * step, axis=1
+    )
+    going_up = going_down = context_here
+    for far in range(1, ways // 2 + 1):
+        going_up = lax.ppermute(going_up, "seq", [(d, (d + 1) % ways) for d in range(ways)])
+        full = lax.dynamic_update_slice_in_dim(full, going_up, (here - far) % ways * step, axis=1)
+        if 2 * far < ways:
+            going_down = lax.ppermute(going_down, "seq", [(d, (d - 1) % ways) for d in range(ways)])
+            full = lax.dynamic_update_slice_in_dim(
+                full, going_down, (here + far) % ways * step, axis=1
+            )
+    context = full
     middle = inputs + matmul(context, wide_proj)
     lowered_two = layer_norm(middle, gain_two, bias_two).astype(LOW)
     hidden_pre = matmul(lowered_two, wide_hidden)

time: 508 us -> 467 us (0.919)
  waiting for transfers between devices: 278 us -> 227 us
  local copies, waits for them, and re-layouts: 38.9 us -> 45.9 us
    all_gather x1 -> x0, waiting for transfers between devices: 39.3 us -> none  [on_device(): context = lax.all_gather(context_here, 'seq', axis=1, tiled=True)]
    ppermute x0 -> x3, waiting for transfers between devices: none -> 20.5 us  [the longest x2 16.5 us: on_device(): lax.ppermute(going_up, 'seq', [(d, (d + 1) % ways) for d in range(ways)])]
    all_gather x1, waiting for transfers between devices: 19.2 us -> 0.01 us  [on_device(): wide_hidden = lax.all_gather(hidden_cols, 'dp', axis=0, tiled=True)]
    all_gather x1, waiting for transfers between devices: 5.78 us -> 0.01 us  [on_device(): wide_proj = lax.all_gather(proj_weight, 'dp', axis=0, tiled=True)]
    dynamic_update_slice x0 -> x3, local copies, waits for them, and re-layouts: none -> 5.33 us  [the longest x2 3.56 us: on_device(): lax.dynamic_update_slice_in_dim(full, going_up, (here - far) % ways * ste...]
    unnamed x123 -> x127, local copies, waits for them, and re-layouts: 16.8 us -> 16.7 us
  transfers between devices with their start and end apart: 13 -> 15, of which waited for: 12 -> 12; matrix products, arithmetic and copies ran while one was open for 20% -> 24% of each run, Pallas kernels for 0% -> 0%
where the time goes in v1:
time: 467 us; the launch traced here: 462 us
  waiting for transfers between devices  227 us (49%)
  blocking collectives  85 us (18%)
  matrix products  48.9 us (10%)
  local copies, waits for them, and re-layouts  45.9 us (10%)
  other arithmetic  34.1 us (7%)
  between operations  15.5 us (3%)
  starting transfers between devices  5.22 us (1%)
    all_gather x3, waiting for transfers between devices, gather_seq(): return lax.all_gather(value, 'seq', axis=0, tiled=True)  88.7 us
    psum x1, blocking collectives, on_device(): norm_sum = lax.psum(norm_terms, ('seq', 'dp'))  41.2 us
    reduce_scatter x1, waiting for transfers between devices, on_device(): lax.psum_scatter(first_terms, 'dp', scatter_dimension=0, tiled=True)  35.1 us
    reduce_scatter x3, waiting for transfers between devices, scatter_seq(): lax.psum_scatter(value.astype(LOW), 'seq', scatter_dimension=0, tiled=True)  32.9 us
    reduce_scatter x1, waiting for transfers between devices, on_device(): lax.psum_scatter(second_terms, 'dp', scatter_dimension=0, tiled=True)  28.1 us
    all_gather x1, blocking collectives, on_device(): second_all = lax.all_gather(second_sum, 'seq', axis=0)  22.1 us
    all_gather x1, waiting for transfers between devices, on_device(): wide_output = lax.all_gather(output_here, 'dp', axis=0, tiled=True)  20.1 us
    unnamed x127, local copies, waits for them, and re-layouts  16.7 us
  transfers between devices with their start and end apart: 15, of which 12 were waited for; matrix products, arithmetic and copies ran while one was open for 24% of the time, Pallas kernels for 0%

profile of v1, /device:TPU:0, one launch (start us, length us, event | category | flops | bytes accessed | tf_op | source)
XLA Modules:
  0.0 462.0 jit_solution(7412180862958080024)
XLA Ops:
  7.3 2.0 copy.123
  10.1 2.3 reshape.268
  12.4 1.2 dynamic-slice_reduce_fusion.1
  15.4 10.3 %all-gather.4 = bf16[8,96,4]{1,2,0:T(4,128)(2,1)S(1)} all-gather(bf16[1,96,4]{1,2,0:T(4,128)(2,1)S(1)} %maximum_bitcast_fusion), channel_id=1, replica_groups=mesh['seq'=4,'dp'=8] {'dp'}, dimensions={0}, use_global_device_ids=true | all-gather | bytes 6912 | tf_op jit(solution)/shard_map/all_gather | solution.py:138
  29.0 11.3 %all_gather.38 = bf16[768,576]{1,0:T(8,128)(2,1)S(1)} all-gather(bf16[96,576]{1,0:T(8,128)(2,1)S(1)} %copy.126), channel_id=1, replica_groups=mesh['seq'=4,'dp'=8] {'dp'}, dimensions={0}, use_global_device_ids=true | all-gather | bytes 995328 | tf_op jit(solution)/shard_map/all_gather | solution.py:141
  40.4 10.3 %all-gather.21.cloned.1.call-done = bf16[1,1024,768]{1,2,0:T(8,128)(2,1)} async-done(((bf16[1,256,768]{1,2,0:T(8,128)(2,1)}), bf16[1,1024,768]{1,2,0:T(8,128)(2,1)}) %all-gather.21.cloned.1.call-update) | async-done | bytes 1572880 | tf_op jit(solution)/shard_map/all_gather | solution.py:35
  50.7 1.8 convert_reduce_fusion
  52.5 1.9 fusion.6
  54.4 1.3 convolution_convert_fusion.4
  55.9 1.4 fusion.88
  57.4 1.5 fusion
  60.9 1.7 fusion.55
  62.6 1.4 broadcast_in_dim.46
  65.7 3.0 collective-permute-start.1
  68.7 10.3 %collective-permute-done = bf16[1024,192]{0,1:T(8,128)(2,1)} collective-permute-done((bf16[1024,192]{0,1:T(8,128)(2,1)}, bf16[1024,192]{0,1:T(8,128)(2,1)}, u32[]{:S(2)}, u32[]{:S(2)}) %collective-permute-start) | collective-permute-done | bytes 393248 | tf_op jit(solution)/shard_map/ppermute | solution.py:160
  79.7 1.8 constant_dynamic-update-slice_fusion.2
  81.5 3.9 collective-permute-done.1
  85.4 1.8 constant_dynamic-update-slice_fusion.1
  87.2 6.2 %collective-permute-done.2 = bf16[1024,192]{0,1:T(8,128)(2,1)} collective-permute-done((bf16[1024,192]{0,1:T(8,128)(2,1)}, bf16[1024,192]{0,1:T(8,128)(2,1)}, u32[]{:S(2)}, u32[]{:S(2)}) %collective-permute-start.2) | collective-permute-done | bytes 393248 | tf_op jit(solution)/shard_map/ppermute | solution.py:160
  93.4 1.8 constant_dynamic-update-slice_fusion
  95.2 3.8 fusion.90
  99.4 1.3 copy-done.3
  100.7 1.7 add_convert_fusion
  102.4 4.8 %fusion.91 = f32[1024,768]{1,0:T(8,128)} fusion(bf16[1024,768]{0,1:T(8,128)(2,1)} %add_convert_fusion, bf16[768,768]{1,0:T(8,128)(2,1)} %all-gather.15.cloned.1.call-done), kind=kOutput, calls=%fused_computation.170 | convolution fusion | flops 1207959552 | bytes 5898240 | tf_op jit(solution)/shard_map/dot_general | solution.py:23
  107.2 20.1 %all-gather.17.cloned.1.call-done = bf16[768,768]{1,0:T(8,128)(2,1)} async-done(((bf16[96,768]{1,0:T(8,128)(2,1)}), bf16[768,768]{1,0:T(8,128)(2,1)}) %all-gather.17.cloned.1.call-update) | async-done | bytes 1179664 | tf_op jit(solution)/shard_map/all_gather | solution.py:144
  127.3 38.5 %all-gather.23.cloned.1.call-done = bf16[1,1024,768]{2,1,0:T(8,128)(2,1)} async-done(((bf16[1,256,768]{2,1,0:T(8,128)(2,1)}), bf16[1,1024,768]{2,1,0:T(8,128)(2,1)}) %all-gather.23.cloned.1.call-update) | async-done | bytes 1572880 | tf_op jit(solution)/shard_map/all_gather | solution.py:35
  165.8 5.6 %fusion.16 = bf16[1024,768]{1,0:T(8,128)(2,1)S(1)} fusion(f32[1024,768]{1,0:T(8,128)} %fusion.91, bf16[768,768]{1,0:T(8,128)(2,1)} %all-gather.17.cloned.1.call-done, bf16[1,1024,768]{2,1,0:T(8,128)(2,1)} %all-gather.23.cloned.1.call-done), kind=kOutput, calls=%fused_computation.26 | convolution fusion | flops 1223688192 | bytes 7471104 | tf_op jit(solution)/shard_map/dot_general | solution.py:31
  172.6 2.6 convolution_convert_fusion.1
  175.2 3.5 convolution_convert_fusion.3
  178.7 1.7 fusion.33
  180.4 1.5 pad_maximum_fusion
  182.0 4.3 copy.156
  186.5 1.9 copy.130
  188.4 1.3 dynamic-slice_reduce_fusion
  190.3 19.2 %reduce-scatter.12.cloned.1.call-done = bf16[256,768]{0,1:T(8,128)(2,1)} async-done(((bf16[1024,768]{0,1:T(8,128)(2,1)}), bf16[256,768]{0,1:T(8,128)(2,1)}) %reduce-scatter.12.cloned.1.call-update) | async-done | bytes 393232 | tf_op jit(solution)/shard_map/reduce_scatter | solution.py:39
  209.5 2.2 multiply_reduce_fusion.3
  211.7 2.3 fusion.67
  214.6 2.4 fusion.70
  217.1 1.3 log_add_fusion.1
  219.2 35.1 %reduce-scatter.18.cloned.1.call-done = bf16[96,1536]{1,0:T(8,128)(2,1)} async-done(((bf16[768,1536]{1,0:T(8,128)(2,1)}), bf16[96,1536]{1,0:T(8,128)(2,1)}) %reduce-scatter.18.cloned.1.call-update) | async-done | bytes 294928 | tf_op jit(solution)/shard_map/reduce_scatter | solution.py:200
  254.4 39.9 %all-gather.19.cloned.1.call-done = bf16[1024,768]{0,1:T(8,128)(2,1)} async-done(((bf16[256,768]{0,1:T(8,128)(2,1)}), bf16[1024,768]{0,1:T(8,128)(2,1)}) %all-gather.19.cloned.1.call-update) | async-done | bytes 1572880 | tf_op jit(solution)/shard_map/all_gather | solution.py:35
  294.3 2.0 convolution_convert_fusion.6
  296.3 1.5 multiply_reduce_fusion.1
  301.2 1.9 multiply_reduce_fusion
  303.2 1.4 multiply_convert_fusion
  305.7 2.2 convolution_convert_fusion.7
  310.7 1.3 convolution_convert_fusion.5
  312.1 1.5 copy.154
  313.7 2.5 convolution_convert_fusion
  316.5 5.0 %convolution_convert_fusion.2 = bf16[1024,768]{0,1:T(8,128)(2,1)} fusion(bf16[768,768]{1,0:T(8,128)(2,1)} %all-gather.17.cloned.1.call-done, f32[1024,768]{1,0:T(8,128)} %fusion.91), kind=kOutput, calls=%fused_computation.50 | convolution fusion | flops 1215823872 | bytes 5898240 | tf_op jit(solution)/shard_map/dot_general | solution.py:23
  323.4 1.2 all-gather.25.cloned.1.call-done
  324.6 2.4 fusion.84
  327.0 1.9 reshape.285
  328.9 2.2 copy.143
  331.1 3.6 reshape.282
  335.9 28.1 %reduce-scatter.16.cloned.1.call-done = bf16[96,768]{1,0:T(8,128)(2,1)} async-done(((bf16[768,768]{1,0:T(8,128)(2,1)}), bf16[96,768]{1,0:T(8,128)(2,1)}) %reduce-scatter.16.cloned.1.call-update) | async-done | bytes 147472 | tf_op jit(solution)/shard_map/reduce_scatter | solution.py:201
  364.0 22.1 %all-gather.2 = bf16[384,768]{1,0:T(8,128)(2,1)S(1)} all-gather(bf16[96,768]{1,0:T(8,128)(2,1)} %reduce-scatter.16.cloned.1.call-done), channel_id=4, replica_groups=mesh['seq'=4,'dp'=8] {'seq'}, dimensions={0}, use_global_device_ids=true | all-gather | bytes 737280 | tf_op jit(solution)/shard_map/all_gather | solution.py:203
  388.1 1.6 copy.140
  389.6 2.9 reshape.280
  392.6 13.7 %reduce-scatter.14.cloned.1.call-done = bf16[256,768]{0,1:T(8,128)(2,1)} async-done(((bf16[1024,768]{0,1:T(8,128)(2,1)}), bf16[256,768]{0,1:T(8,128)(2,1)}) %reduce-scatter.14.cloned.1.call-update) | async-done | bytes 393232 | tf_op jit(solution)/shard_map/reduce_scatter | solution.py:39
  406.2 1.4 fusion.66
  407.7 1.5 fusion.68
  409.3 41.2 %psum.7 = f32[4,768]{1,0:T(4,128)S(1)} all-reduce(f32[4,768]{1,0:T(4,128)S(1)} %pad_maximum_fusion.6), channel_id=1, replica_groups=mesh['seq'=4,'dp'=8] {'seq','dp'}, use_global_device_ids=true, to_apply=%region_27.28 | all-reduce | flops 3072 | bytes 24576 | tf_op jit(solution)/shard_map/psum | solution.py:223
  451.1 2.0 fusion.73
  (207 shorter events, 29.1 us)
Async XLA Ops:
  7.2 7.4 %copy-start = (bf16[384,768]{1,0:T(8,128)(2,1)S(1)}, bf16[384,768]{1,0:T(8,128)(2,1)}, u32[]{:S(2)}) copy-start(bf16[384,768]{1,0:T(8,128)(2,1)} %param.14) | copy-start | bytes 1769476
  7.2 8.2 %copy-start.50 = (bf16[96]{0:T(256)(128)(2,1)S(1)}, bf16[96]{0:T(256)(128)(2,1)}, u32[]{:S(2)}) copy-start(bf16[96]{0:T(256)(128)(2,1)} %param.18) | copy-start | bytes 580
  7.2 8.2 %copy-start.51 = (bf16[96]{0:T(256)(128)(2,1)S(1)}, bf16[96]{0:T(256)(128)(2,1)}, u32[]{:S(2)}) copy-start(bf16[96]{0:T(256)(128)(2,1)} %param.17) | copy-start | bytes 580
  7.2 8.2 %copy-start.52 = (bf16[96]{0:T(256)(128)(2,1)S(1)}, bf16[96]{0:T(256)(128)(2,1)}, u32[]{:S(2)}) copy-start(bf16[96]{0:T(256)(128)(2,1)} %param.16) | copy-start | bytes 580
  7.2 8.2 %copy-start.53 = (bf16[96]{0:T(256)(128)(2,1)S(1)}, bf16[96]{0:T(256)(128)(2,1)}, u32[]{:S(2)}) copy-start(bf16[96]{0:T(256)(128)(2,1)} %param.15) | copy-start | bytes 580
  7.2 20.5 %copy-start.22 = (bf16[96,2304]{1,0:T(8,128)(2,1)S(1)}, bf16[96,2304]{1,0:T(8,128)(2,1)}, u32[]{:S(2)}) copy-start(bf16[96,2304]{1,0:T(8,128)(2,1)} %param.11) | copy-start | bytes 1327108
  7.2 43.4 %all-gather.21.cloned.1.call-start = ((), (), s32[]{:S(2)}) async-start(), calls=%async_computation.12 | async-start | bytes 1966080 | tf_op jit(solution)/shard_map/all_gather | solution.py:35
  9.3 85.9 %all-gather.13.cloned.1.call-start = ((), (), s32[]{:S(2)}) async-start(), calls=%async_computation.5 | async-start | bytes 1327104 | tf_op jit(solution)/shard_map/all_gather | solution.py:142
  10.1 92.3 %all-gather.15.cloned.1.call-start = ((), (), s32[]{:S(2)}) async-start(), calls=%async_computation.6 | async-start | bytes 1327104 | tf_op jit(solution)/shard_map/all_gather | solution.py:143
  14.5 112.7 %all-gather.17.cloned.1.call-start = ((), (), s32[]{:S(2)}) async-start(), calls=%async_computation.7 | async-start | bytes 1327104 | tf_op jit(solution)/shard_map/all_gather | solution.py:144
  15.3 150.5 %all-gather.23.cloned.1.call-start = ((), (), s32[]{:S(2)}) async-start(), calls=%async_computation.13 | async-start | bytes 1966080 | tf_op jit(solution)/shard_map/all_gather | solution.py:35
  26.5 27.9 %copy-start.46 = (f32[768]{0:T(1024)}, f32[768]{0:T(1024)S(1)}, u32[]{:S(2)}) copy-start(f32[768]{0:T(1024)S(1)} %get-tuple-element.82) | copy-start | bytes 9220
  40.4 15.3 %copy-start.18 = (bf16[768,576]{1,0:T(8,128)(2,1)}, bf16[768,576]{1,0:T(8,128)(2,1)S(1)}, u32[]{:S(2)}) copy-start(bf16[768,576]{1,0:T(8,128)(2,1)S(1)} %all_gather.38) | copy-start | bytes 2654212
  50.7 3.7 copy-start.5
  52.5 3.3 copy-start.35
  55.8 1.6 copy-start.9
  55.8 3.1 copy-start.11
  55.8 3.1 copy-start.13
  55.8 4.3 copy-start.20
  55.9 5.0 %copy-start.15 = (bf16[1024,192]{0,1:T(8,128)(2,1)}, bf16[1024,192]{0,1:T(8,128)(2,1)S(1)}, u32[]{:S(2)}) copy-start(bf16[1024,192]{0,1:T(8,128)(2,1)S(1)} %get-tuple-element.93) | copy-start | bytes 1179652
  57.4 3.5 copy-start.2
  57.4 3.5 copy-start.28
  57.4 1.5 copy-start.17
  58.9 2.0 copy-start.29
  64.9 14.2 %collective-permute-start = (bf16[1024,192]{0,1:T(8,128)(2,1)}, bf16[1024,192]{0,1:T(8,128)(2,1)}, u32[]{:S(2)}, u32[]{:S(2)}) collective-permute-start(bf16[1024,192]{0,1:T(8,128)(2,1)} %get-tuple-element.96), channel_id=1, source_target_pairs={{0,8},{8,16},{16,24},{24,0},{1,9},{9,17},{17,25},{25,1},{2,10},{10... | collective-permute-start | bytes 1179656 | tf_op jit(solution)/shard_map/ppermute | solution.py:160
  65.7 19.7 %collective-permute-start.1 = (bf16[1024,192]{0,1:T(8,128)(2,1)}, bf16[1024,192]{0,1:T(8,128)(2,1)}, u32[]{:S(2)}, u32[]{:S(2)}) collective-permute-start(bf16[1024,192]{0,1:T(8,128)(2,1)} %get-tuple-element.96), channel_id=1, source_target_pairs={{0,24},{8,0},{16,8},{24,16},{1,25},{9,1},{17,9},{25,17},{2,26},{10... | collective-permute-start | bytes 1179656 | tf_op jit(solution)/shard_map/ppermute | solution.py:163
  79.1 14.3 %collective-permute-start.2 = (bf16[1024,192]{0,1:T(8,128)(2,1)}, bf16[1024,192]{0,1:T(8,128)(2,1)}, u32[]{:S(2)}, u32[]{:S(2)}) collective-permute-start(bf16[1024,192]{0,1:T(8,128)(2,1)} %collective-permute-done), channel_id=1, source_target_pairs={{0,8},{8,16},{16,24},{24,0},{1,9},{9,17},{17,25},{25,1},{2,10},{10... | collective-permute-start | bytes 1179656 | tf_op jit(solution)/shard_map/ppermute | solution.py:160
  79.1 130.4 %reduce-scatter.12.cloned.1.call-start = ((), (), s32[]{:S(2)}) async-start(), calls=%async_computation.9 | async-start | bytes 1966080 | tf_op jit(solution)/shard_map/reduce_scatter | solution.py:39
  99.0 1.7 copy-start.3
  99.0 1.7 copy-start.32
  165.8 6.8 %copy-start.55 = (bf16[768,768]{1,0:T(8,128)(2,1)S(1)}, bf16[768,768]{1,0:T(8,128)(2,1)}, u32[]{:S(2)}) copy-start(bf16[768,768]{1,0:T(8,128)(2,1)} %all-gather.15.cloned.1.call-done) | copy-start | bytes 3538948
  175.1 79.2 %reduce-scatter.18.cloned.1.call-start = ((), (), s32[]{:S(2)}) async-start(), calls=%async_computation.16 | async-start | bytes 2654208 | tf_op jit(solution)/shard_map/reduce_scatter | solution.py:200
  175.2 3.5 copy-start.54
  175.2 3.5 copy-start.56
  186.3 108.0 %all-gather.19.cloned.1.call-start = ((), (), s32[]{:S(2)}) async-start(), calls=%async_computation.10 | async-start | bytes 1966080 | tf_op jit(solution)/shard_map/all_gather | solution.py:35
  211.7 2.3 copy-start.38
  211.7 2.3 copy-start.40
  217.1 107.5 %all-gather.25.cloned.1.call-start = ((), (), s32[]{:S(2)}) async-start(), calls=%async_computation.14 | async-start | bytes 1474560 | tf_op jit(solution)/shard_map/all_gather | solution.py:202
  254.3 109.6 %reduce-scatter.16.cloned.1.call-start = ((), (), s32[]{:S(2)}) async-start(), calls=%async_computation.15 | async-start | bytes 1327104 | tf_op jit(solution)/shard_map/reduce_scatter | solution.py:201
  294.3 2.1 copy-start.21
  297.8 2.4 slice-start
  297.9 3.1 slice-start.1
  298.9 2.3 copy-start.16
  299.3 11.1 %copy-start.25 = (bf16[3,64,512]{2,1,0:T(8,128)(2,1)}, bf16[3,64,512]{2,1,0:T(8,128)(2,1)S(1)}, u32[]{:S(2)}) copy-start(bf16[3,64,512]{2,1,0:T(8,128)(2,1)S(1)} %fusion.52) | copy-start | bytes 589828
  304.6 3.4 copy-start.10
  305.7 4.8 %copy-start.23 = (bf16[3,64,512]{2,1,0:T(8,128)(2,1)}, bf16[3,64,512]{2,1,0:T(8,128)(2,1)S(1)}, u32[]{:S(2)}) copy-start(bf16[3,64,512]{2,1,0:T(8,128)(2,1)S(1)} %fusion.53) | copy-start | bytes 589828
  312.0 1.7 copy-start.19
  312.0 1.7 copy-start.24
  312.0 1.7 copy-start.26
  313.6 92.6 %reduce-scatter.14.cloned.1.call-start = ((), (), s32[]{:S(2)}) async-start(), calls=%async_computation.11 | async-start | bytes 1966080 | tf_op jit(solution)/shard_map/reduce_scatter | solution.py:39
  316.2 5.3 %copy-start.4 = (bf16[1,256,768]{1,2,0:T(8,128)(2,1)S(1)}, bf16[1,256,768]{1,2,0:T(8,128)(2,1)}, u32[]{:S(2)}) copy-start(bf16[1,256,768]{1,2,0:T(8,128)(2,1)} %copy.123) | copy-start | bytes 1179652
  316.2 6.0 %copy-start.33 = (f32[768]{0:T(1024)S(1)}, f32[768]{0:T(1024)}, u32[]{:S(2)}) copy-start(f32[768]{0:T(1024)} %get-tuple-element.79) | copy-start | bytes 9220
  316.2 6.6 %copy-start.34 = (f32[768]{0:T(1024)S(1)}, f32[768]{0:T(1024)}, u32[]{:S(2)}) copy-start(f32[768]{0:T(1024)} %get-tuple-element.70) | copy-start | bytes 9220
  316.2 134.8 %reduce-scatter.10.cloned.1.call-start = ((), (), s32[]{:S(2)}) async-start(), calls=%async_computation.8 | async-start | bytes 1966080 | tf_op jit(solution)/shard_map/reduce_scatter | solution.py:39
  388.0 18.3 %copy-start.37 = (f32[256]{0:T(256)S(1)}, f32[256]{0:T(256)}, u32[]{:S(2)}) copy-start(f32[256]{0:T(256)} %broadcast_multiply_fusion.2) | copy-start | bytes 3076
  388.0 21.2 %copy-start.42 = (f32[1,768]{1,0:T(1,128)S(1)}, f32[1,768]{1,0:T(1,128)}, u32[]{:S(2)}) copy-start(f32[1,768]{1,0:T(1,128)} %reshape.279) | copy-start | bytes 9220
  388.0 21.2 %copy-start.43 = (f32[1,768]{1,0:T(1,128)S(1)}, f32[1,768]{1,0:T(1,128)}, u32[]{:S(2)}) copy-start(f32[1,768]{1,0:T(1,128)} %reshape.278) | copy-start | bytes 9220
  388.0 63.1 %copy-start.7 = (bf16[256,768]{0,1:T(8,128)(2,1)S(1)}, bf16[256,768]{0,1:T(8,128)(2,1)}, u32[]{:S(2)}) copy-start(bf16[256,768]{0,1:T(8,128)(2,1)} %reduce-scatter.12.cloned.1.call-done) | copy-start | bytes 1179652
  388.0 63.1 %copy-start.8 = (bf16[1,256,768]{1,2,0:T(8,128)(2,1)S(1)}, bf16[1,256,768]{1,2,0:T(8,128)(2,1)}, u32[]{:S(2)}) copy-start(bf16[1,256,768]{1,2,0:T(8,128)(2,1)} %copy.130) | copy-start | bytes 1179652
  388.0 63.1 %copy-start.31 = (f32[256]{0:T(256)S(1)}, f32[256]{0:T(256)}, u32[]{:S(2)}) copy-start(f32[256]{0:T(256)} %broadcast_multiply_fusion.3) | copy-start | bytes 3076
  388.0 63.1 %copy-start.39 = (f32[256]{0:T(256)S(1)}, f32[256]{0:T(256)}, u32[]{:S(2)}) copy-start(f32[256]{0:T(256)} %copy-done.38) | copy-start | bytes 3076
  388.0 63.1 %copy-start.41 = (f32[256]{0:T(256)S(1)}, f32[256]{0:T(256)}, u32[]{:S(2)}) copy-start(f32[256]{0:T(256)} %copy-done.40) | copy-start | bytes 3076
  388.0 63.1 %copy-start.45 = (f32[256]{0:T(256)S(1)}, f32[256]{0:T(256)}, u32[]{:S(2)}) copy-start(f32[256]{0:T(256)} %copy-done.44) | copy-start | bytes 3076
  406.2 48.7 %copy-start.1 = (bf16[384,768]{1,0:T(8,128)(2,1)S(1)}, bf16[384,768]{1,0:T(8,128)(2,1)}, u32[]{:S(2)}) copy-start(bf16[384,768]{1,0:T(8,128)(2,1)} %param.14) | copy-start | bytes 1769476
  (11 other events, 13.6 us)
Sparse Core Ops, SparseCore 0:
  10.2 40.3 all-gather.20
  52.5 22.2 all-gather.12
  77.3 24.0 all-gather.14
  103.2 24.0 all-gather.16
  128.7 37.0 all-gather.22
  175.3 34.1 reduce-scatter.11
  212.8 41.4 reduce-scatter.17
  256.5 37.6 all-gather.18
  295.9 28.6 all-gather.24
  328.0 35.8 reduce-scatter.15
  366.3 39.8 reduce-scatter.13
  408.4 35.1 reduce-scatter.9
